TPU v7x, 1024 devices: a whole 8x8x8 slice. The times are simulated.
1024 devices in a mesh: dp: 64 (over z, y_lo, core), tensor: 16 (over x, y_hi).
Axes of the slice: x: 8, y: 8 (y_hi: 2, y_lo: 4; y = y_hi * 4 + y_lo), z: 8, core: 2. Of those that a mesh axis runs over, the one named last changes fastest.
Arguments:
- tokens: bfloat16 [16384, 8192], P('dp', 'tensor'), may hold values from -6 to 6
- weight: bfloat16 [1024, 8192], P('dp', 'tensor'), may hold values from -0.0625 to 0.0625
- cotangent: bfloat16 [16384, 1024], P(('dp', 'tensor')), may hold values from -24 to 24
Outputs:
- outputs: bfloat16 [16384, 1024], P(('dp', 'tensor'))
- grad_tokens: bfloat16 [16384, 8192], P('dp', 'tensor')
- weight_grad: float32 [1024, 8192], P('dp', 'tensor')
All inputs are finite; a program needn't handle non-finite values.
Results may differ from a plain program's by a relative error of at most 0.019.
Values may be sent and summed in bfloat16 or wider, within the bound.
A program may use at most 32 MiB of HBM per device.

v0:
```python
import jax
import jax.numpy as jnp
from jax import lax
from jax.sharding import PartitionSpec as P


def swapped(value, axis, distance):
    mask = 2**distance
    pairs = [(source, source ^ mask) for source in range(lax.axis_size(axis))]
    return lax.ppermute(value, axis, pairs)


def signs_table(order_size):
    bit_count = order_size.bit_length() - 1
    positions = lax.iota(jnp.int32, order_size)
    parity = jnp.zeros((order_size, order_size), jnp.int32)
    for bit_number in range(bit_count):
        parity = parity + (positions[:, None] >> bit_number & 1) * (
            positions[None, :] >> bit_number & 1
        )
    return (1 - 2 * (parity % 2)).astype(jnp.bfloat16)


def rotate(values):
    row_count, width = values.shape
    blended = jnp.dot(values, signs_table(width), preferred_element_type=jnp.float32)
    blended = (blended * jnp.float32(width ** (-0.5))).astype(jnp.bfloat16)
    blocks = lax.axis_size("tensor")
    section_total = blocks.bit_length() - 1
    my_index = lax.axis_index("tensor")
    for section_number in range(section_total):
        partner = swapped(blended, "tensor", section_number)
        upper_side = my_index >> section_number & 1 == 1
        own_values = blended.astype(jnp.float32)
        partner_values = partner.astype(jnp.float32)
        combined = jnp.where(upper_side, partner_values - own_values, own_values + partner_values)
        blended = (combined * jnp.float32(0.5**0.5)).astype(jnp.bfloat16)
    return blended


def on_device(tokens, weight, cotangent):
    rotated = rotate(tokens)
    whole_weight = lax.all_gather(weight, "dp", axis=0, tiled=True)
    partial_value = lax.dot_general(
        rotated, whole_weight, (((1,), (1,)), ((), ())), preferred_element_type=jnp.float32
    ).astype(jnp.bfloat16)
    partial_value = lax.optimization_barrier(partial_value)
    outputs = lax.psum_scatter(
        partial_value.astype(jnp.float32).astype(jnp.bfloat16),
        "tensor",
        scatter_dimension=0,
        tiled=True,
    )
    gathered_grad = lax.all_gather(cotangent, "tensor", axis=0, tiled=True)
    grad_sum = jnp.dot(gathered_grad, whole_weight, preferred_element_type=jnp.float32)
    grad_tokens = rotate(grad_sum.astype(jnp.bfloat16))
    norm_scale = jnp.float32((tokens.shape[0] * lax.axis_size("dp")) ** (-0.5))
    weight_grad = lax.psum_scatter(
        lax.dot_general(
            gathered_grad, rotated, (((0,), (0,)), ((), ())), preferred_element_type=jnp.float32
        )
        * norm_scale,
        "dp",
        scatter_dimension=0,
        tiled=True,
    )
    return (outputs, grad_tokens, weight_grad)


def solution(mesh):
    return jax.shard_map(
        on_device,
        mesh=mesh,
        in_specs=(P("dp", "tensor"), P("dp", "tensor"), P(("dp", "tensor"), None)),
        out_specs=(P(("dp", "tensor"), None), P("dp", "tensor"), P("dp", "tensor")),
        check_vma=False,
    )
```

profile of v0, /device:TPU:2, one launch (start us, length us, event | category | flops | bytes accessed | tf_op | source)
XLA Modules:
  0.0 666.4 jit_solution(15831761385895913733)
XLA Ops:
  8.1 1.5 fusion.2
  9.6 8.2 %collective-permute-start = (bf16[256,512]{0,1:T(8,128)(2,1)S(1)}, bf16[256,512]{0,1:T(8,128)(2,1)S(1)}, u32[]{:S(2)}, u32[]{:S(2)}) collective-permute-start(bf16[256,512]{0,1:T(8,128)(2,1)S(1)} %fusion.2), channel_id=1, source_target_pairs={{0,1},{1,0},{2,3},{3,2},{4,5},{5,4},{6,7},{7,6},{8,9},{9,8},{10,11... | collective-permute-start | bytes 786440 | tf_op jit(solution)/shard_map/ppermute | solution.py:10
  17.8 7.9 %collective-permute-done = bf16[256,512]{0,1:T(8,128)(2,1)S(1)} collective-permute-done((bf16[256,512]{0,1:T(8,128)(2,1)S(1)}, bf16[256,512]{0,1:T(8,128)(2,1)S(1)}, u32[]{:S(2)}, u32[]{:S(2)}) %collective-permute-start) | collective-permute-done | bytes 262176 | tf_op jit(solution)/shard_map/ppermute | solution.py:10
  25.8 11.2 %collective-permute-start.1 = (bf16[256,512]{0,1:T(8,128)(2,1)S(1)}, bf16[256,512]{0,1:T(8,128)(2,1)S(1)}, u32[]{:S(2)}, u32[]{:S(2)}) collective-permute-start(bf16[256,512]{0,1:T(8,128)(2,1)S(1)} %fusion.9), channel_id=1, source_target_pairs={{0,2},{1,3},{2,0},{3,1},{4,6},{5,7},{6,4},{7,5},{8,10},{9,11},{10,... | collective-permute-start | bytes 786440 | tf_op jit(solution)/shard_map/ppermute | solution.py:10
  37.0 6.9 %collective-permute-done.1 = bf16[256,512]{0,1:T(8,128)(2,1)S(1)} collective-permute-done((bf16[256,512]{0,1:T(8,128)(2,1)S(1)}, bf16[256,512]{0,1:T(8,128)(2,1)S(1)}, u32[]{:S(2)}, u32[]{:S(2)}) %collective-permute-start.1) | collective-permute-done | bytes 262176 | tf_op jit(solution)/shard_map/ppermute | solution.py:10
  44.0 1.9 collective-permute-start.2
  45.9 7.3 %collective-permute-done.2 = bf16[256,512]{0,1:T(8,128)(2,1)S(1)} collective-permute-done((bf16[256,512]{0,1:T(8,128)(2,1)S(1)}, bf16[256,512]{0,1:T(8,128)(2,1)S(1)}, u32[]{:S(2)}, u32[]{:S(2)}) %collective-permute-start.2) | collective-permute-done | bytes 262176 | tf_op jit(solution)/shard_map/ppermute | solution.py:10
  53.4 1.9 collective-permute-start.3
  55.3 13.0 %collective-permute-done.3 = bf16[256,512]{0,1:T(8,128)(2,1)S(1)} collective-permute-done((bf16[256,512]{0,1:T(8,128)(2,1)S(1)}, bf16[256,512]{0,1:T(8,128)(2,1)S(1)}, u32[]{:S(2)}, u32[]{:S(2)}) %collective-permute-start.3) | collective-permute-done | bytes 262176 | tf_op jit(solution)/shard_map/ppermute | solution.py:10
  68.3 72.9 %all-gather.2.cloned.1.call-done = bf16[1024,512]{1,0:T(8,128)(2,1)} async-done(((bf16[16,512]{1,0:T(8,128)(2,1)}), bf16[1024,512]{1,0:T(8,128)(2,1)}) %all-gather.2.cloned.1.call-update) | async-done | bytes 1048592 | tf_op jit(solution)/shard_map/all_gather | solution.py:43
  141.2 2.5 convolution_convert_fusion
  143.8 57.1 %all_gather.7 = bf16[256,1024]{1,0:T(8,128)(2,1)S(1)} all-gather(bf16[16,1024]{1,0:T(8,128)(2,1)S(1)} %copy-done.1), channel_id=1, replica_groups=mesh['dp'=64,'tensor'=16] {'tensor'}, dimensions={0}, use_global_device_ids=true | all-gather | bytes 557056 | tf_op jit(solution)/shard_map/all_gather | solution.py:54
  201.4 1.8 copy.13
  204.5 1.7 fusion.1
  206.2 1.9 collective-permute-start.4
  208.2 13.2 %collective-permute-done.4 = bf16[256,512]{0,1:T(8,128)(2,1)S(1)} collective-permute-done((bf16[256,512]{0,1:T(8,128)(2,1)S(1)}, bf16[256,512]{0,1:T(8,128)(2,1)S(1)}, u32[]{:S(2)}, u32[]{:S(2)}) %collective-permute-start.4) | collective-permute-done | bytes 262176 | tf_op jit(solution)/shard_map/ppermute | solution.py:10
  221.5 5.9 collective-permute-start.5
  227.4 4.3 collective-permute-done.5
  231.9 1.9 collective-permute-start.6
  233.8 11.4 %collective-permute-done.6 = bf16[256,512]{0,1:T(8,128)(2,1)S(1)} collective-permute-done((bf16[256,512]{0,1:T(8,128)(2,1)S(1)}, bf16[256,512]{0,1:T(8,128)(2,1)S(1)}, u32[]{:S(2)}, u32[]{:S(2)}) %collective-permute-start.6) | collective-permute-done | bytes 262176 | tf_op jit(solution)/shard_map/ppermute | solution.py:10
  245.3 5.2 collective-permute-start.7
  250.5 7.0 %collective-permute-done.7 = bf16[256,512]{0,1:T(8,128)(2,1)S(1)} collective-permute-done((bf16[256,512]{0,1:T(8,128)(2,1)S(1)}, bf16[256,512]{0,1:T(8,128)(2,1)S(1)}, u32[]{:S(2)}, u32[]{:S(2)}) %collective-permute-start.7) | collective-permute-done | bytes 262176 | tf_op jit(solution)/shard_map/ppermute | solution.py:10
  258.5 112.1 %reduce-scatter.5.cloned.1.call-done = bf16[16,1024]{1,0:T(8,128)(2,1)} async-done(((bf16[256,1024]{1,0:T(8,128)(2,1)}), bf16[16,1024]{1,0:T(8,128)(2,1)}) %reduce-scatter.5.cloned.1.call-update) | async-done | bytes 32784 | tf_op jit(solution)/shard_map/reduce_scatter | solution.py:48
  370.7 289.2 %reduce-scatter.7.cloned.1.call-done = f32[16,512]{1,0:T(8,128)} async-done(((f32[1024,512]{1,0:T(8,128)}), f32[16,512]{1,0:T(8,128)}) %reduce-scatter.7.cloned.1.call-update) | async-done | bytes 32784
  (26 shorter events, 4.3 us)
Async XLA Ops:
  7.2 1.0 copy-start
  7.2 134.0 %all-gather.2.cloned.1.call-start = ((), (), s32[]{:S(2)}) async-start(), calls=%async_computation.2 | async-start | bytes 1064960 | tf_op jit(solution)/shard_map/all_gather | solution.py:43
  7.9 362.7 %reduce-scatter.5.cloned.1.call-start = ((), (), s32[]{:S(2)}) async-start(), calls=%async_computation.3 | async-start | bytes 557056 | tf_op jit(solution)/shard_map/reduce_scatter | solution.py:48
  9.6 16.1 %collective-permute-start = (bf16[256,512]{0,1:T(8,128)(2,1)S(1)}, bf16[256,512]{0,1:T(8,128)(2,1)S(1)}, u32[]{:S(2)}, u32[]{:S(2)}) collective-permute-start(bf16[256,512]{0,1:T(8,128)(2,1)S(1)} %fusion.2), channel_id=1, source_target_pairs={{0,1},{1,0},{2,3},{3,2},{4,5},{5,4},{6,7},{7,6},{8,9},{9,8},{10,11... | collective-permute-start | bytes 786440 | tf_op jit(solution)/shard_map/ppermute | solution.py:10
  25.8 18.1 %collective-permute-start.1 = (bf16[256,512]{0,1:T(8,128)(2,1)S(1)}, bf16[256,512]{0,1:T(8,128)(2,1)S(1)}, u32[]{:S(2)}, u32[]{:S(2)}) collective-permute-start(bf16[256,512]{0,1:T(8,128)(2,1)S(1)} %fusion.9), channel_id=1, source_target_pairs={{0,2},{1,3},{2,0},{3,1},{4,6},{5,7},{6,4},{7,5},{8,10},{9,11},{10,... | collective-permute-start | bytes 786440 | tf_op jit(solution)/shard_map/ppermute | solution.py:10
  37.0 106.8 %copy-start.1 = (bf16[16,1024]{1,0:T(8,128)(2,1)S(1)}, bf16[16,1024]{1,0:T(8,128)(2,1)}, u32[]{:S(2)}) copy-start(bf16[16,1024]{1,0:T(8,128)(2,1)} %param.5) | copy-start | bytes 98308
  44.0 9.3 %collective-permute-start.2 = (bf16[256,512]{0,1:T(8,128)(2,1)S(1)}, bf16[256,512]{0,1:T(8,128)(2,1)S(1)}, u32[]{:S(2)}, u32[]{:S(2)}) collective-permute-start(bf16[256,512]{0,1:T(8,128)(2,1)S(1)} %fusion.12), channel_id=1, source_target_pairs={{0,4},{1,5},{2,6},{3,7},{4,0},{5,1},{6,2},{7,3},{8,12},{9,13},{10,... | collective-permute-start | bytes 786440 | tf_op jit(solution)/shard_map/ppermute | solution.py:10
  53.4 14.9 %collective-permute-start.3 = (bf16[256,512]{0,1:T(8,128)(2,1)S(1)}, bf16[256,512]{0,1:T(8,128)(2,1)S(1)}, u32[]{:S(2)}, u32[]{:S(2)}) collective-permute-start(bf16[256,512]{0,1:T(8,128)(2,1)S(1)} %fusion.15), channel_id=1, source_target_pairs={{0,8},{1,9},{2,10},{3,11},{4,12},{5,13},{6,14},{7,15},{8,0},{9,1},... | collective-permute-start | bytes 786440 | tf_op jit(solution)/shard_map/ppermute | solution.py:10
  143.8 516.1 %reduce-scatter.7.cloned.1.call-start = ((), (), s32[]{:S(2)}) async-start(), calls=%async_computation.4 | async-start | bytes 2129920
  203.3 1.2 copy-start.2
  206.2 15.1 %collective-permute-start.4 = (bf16[256,512]{0,1:T(8,128)(2,1)S(1)}, bf16[256,512]{0,1:T(8,128)(2,1)S(1)}, u32[]{:S(2)}, u32[]{:S(2)}) collective-permute-start(bf16[256,512]{0,1:T(8,128)(2,1)S(1)} %fusion.1), channel_id=1, source_target_pairs={{0,1},{1,0},{2,3},{3,2},{4,5},{5,4},{6,7},{7,6},{8,9},{9,8},{10,11... | collective-permute-start | bytes 786440 | tf_op jit(solution)/shard_map/ppermute | solution.py:10
  221.5 10.3 %collective-permute-start.5 = (bf16[256,512]{0,1:T(8,128)(2,1)S(1)}, bf16[256,512]{0,1:T(8,128)(2,1)S(1)}, u32[]{:S(2)}, u32[]{:S(2)}) collective-permute-start(bf16[256,512]{0,1:T(8,128)(2,1)S(1)} %fusion.21), channel_id=1, source_target_pairs={{0,2},{1,3},{2,0},{3,1},{4,6},{5,7},{6,4},{7,5},{8,10},{9,11},{10,... | collective-permute-start | bytes 786440 | tf_op jit(solution)/shard_map/ppermute | solution.py:10
  231.9 13.3 %collective-permute-start.6 = (bf16[256,512]{0,1:T(8,128)(2,1)S(1)}, bf16[256,512]{0,1:T(8,128)(2,1)S(1)}, u32[]{:S(2)}, u32[]{:S(2)}) collective-permute-start(bf16[256,512]{0,1:T(8,128)(2,1)S(1)} %fusion.24), channel_id=1, source_target_pairs={{0,4},{1,5},{2,6},{3,7},{4,0},{5,1},{6,2},{7,3},{8,12},{9,13},{10,... | collective-permute-start | bytes 786440 | tf_op jit(solution)/shard_map/ppermute | solution.py:10
  245.3 12.3 %collective-permute-start.7 = (bf16[256,512]{0,1:T(8,128)(2,1)S(1)}, bf16[256,512]{0,1:T(8,128)(2,1)S(1)}, u32[]{:S(2)}, u32[]{:S(2)}) collective-permute-start(bf16[256,512]{0,1:T(8,128)(2,1)S(1)} %fusion.27), channel_id=1, source_target_pairs={{0,8},{1,9},{2,10},{3,11},{4,12},{5,13},{6,14},{7,15},{8,0},{9,1},... | collective-permute-start | bytes 786440 | tf_op jit(solution)/shard_map/ppermute | solution.py:10
Sparse Core Ops, SparseCore 0:
  10.7 130.4 all-gather.1
  147.4 223.1 reduce-scatter.4
  375.0 284.8 reduce-scatter.6
where the time goes:
time: 667 us; the launch traced here: 666 us
  waiting for transfers between devices  546 us (82%)
  blocking collectives  57.1 us (9%)
  starting transfers between devices  38.3 us (6%)
  between operations  13.9 us (2%)
    unnamed x4, waiting for transfers between devices  290 us
    reduce_scatter x1, waiting for transfers between devices, on_device(): lax.psum_scatter(partial_value.astype(jnp.float32).astype(jnp.bfloat16),...  112 us
    all_gather x1, waiting for transfers between devices, on_device(): whole_weight = lax.all_gather(weight, 'dp', axis=0, tiled=True)  72.9 us
    ppermute x8, waiting for transfers between devices, swapped(): return lax.ppermute(value, axis, pairs)  71 us
    all_gather x1, blocking collectives, on_device(): gathered_grad = lax.all_gather(cotangent, 'tensor', axis=0, tiled=True)  57.1 us
    ppermute x8, starting transfers between devices, swapped(): return lax.ppermute(value, axis, pairs)  38.2 us
  transfers between devices with their start and end apart: 11, of which 11 were waited for; matrix products, arithmetic and copies ran while one was open for 1% of the time, Pallas kernels for 0%

commit v1 on v0

v1 whole, which is shorter than its diff:
```python
import functools

import jax
import jax.numpy as jnp
from jax import lax
from jax.experimental import pallas as pl
from jax.experimental.pallas import tpu as pltpu
from jax.sharding import PartitionSpec as P

Z, YL, NC = 8, 4, 2
X, YH = 8, 2
K = 16
INTERPRET = False
F32, BF16 = jnp.float32, jnp.bfloat16


def signs_table(width):
    bits = lax.broadcasted_iota(jnp.int32, (width, width), 0) & lax.broadcasted_iota(
        jnp.int32, (width, width), 1
    )
    for shift in (8, 4, 2, 1):
        bits = bits ^ (bits >> shift)
    return (1 - 2 * (bits & 1)).astype(F32).astype(BF16)


def sign(a, b):
    bits = a & b
    bits = bits ^ (bits >> 2)
    bits = bits ^ (bits >> 1)
    return (1 - 2 * (bits & 1)).astype(F32)


def kernel(
    norm,
    tok, wgt, cot,
    out, gtok, gwgt,
    tbuf, trot, signs, wx, wy, wall, call, pbuf, pcore, psum, prz, py, pry, px,
    obuf, orx, oy, ory, obuf_out, gbuf, gwbuf,
    lsem, wx_s, wx_r, wy_s, wy_r, wz_s, wz_r, wc_s, wc_r, cy_s, cy_r, ca_s, ca_r, cb_s, cb_r,
    pc_s, pc_r, pz_s, pz_r, py_s, py_r, px_s, px_r, ox_s, ox_r, oy_s, oy_r,
):
    width = tbuf.shape[1]
    kv = cot.shape[1]
    group = YL * NC * K
    d, t = lax.axis_index("dp"), lax.axis_index("tensor")
    z, yl, c = d // (YL * NC), (d // NC) % YL, d % NC
    x, yh = t // YH, t % YH
    yy = yh * YL + yl
    NY = YL * YH

    def at_x(r):
        return {"dp": d, "tensor": ((x + r) % X) * YH + yh}

    def at_z(r):
        return {"dp": (((z + r) % Z) * YL + yl) * NC + c, "tensor": t}

    def at_y(r):
        v = (yy + r) % NY
        return {"dp": (z * YL + v % YL) * NC + c, "tensor": x * YH + v // YL}

    at_core = {"dp": (z * YL + yl) * NC + (1 - c), "tensor": t}

    def remote(src, dst, s, r, where):
        return pltpu.make_async_remote_copy(
            src_ref=src, dst_ref=dst, send_sem=s, recv_sem=r,
            device_id=where, device_id_type=pl.DeviceIdType.MESH,
        )

    sends = []

    def send(src, dst, s, r, where):
        copy = remote(src, dst, s, r, where)
        copy.start()
        sends.append(copy)

    def wait_in(dst, s, r):
        remote(dst, dst, s, r, at_core).wait_recv()

    load_w = pltpu.make_async_copy(wgt, wx.at[0], lsem.at[0])
    load_c = pltpu.make_async_copy(cot, call.at[x, yh], lsem.at[1])
    load_t = pltpu.make_async_copy(tok, tbuf, lsem.at[2])
    load_w.start()
    load_c.start()
    load_t.start()

    peers = (
        [at_x(r) for r in range(1, X)]
        + [at_y(r) for r in range(1, NY)]
        + [at_z(r) for r in range(1, Z)]
        + [at_core]
    )
    barrier = pltpu.get_barrier_semaphore()
    for peer in peers:
        pl.semaphore_signal(barrier, inc=1, device_id=peer, device_id_type=pl.DeviceIdType.MESH)
    signs[...] = signs_table(width)
    load_w.wait()
    load_c.wait()
    pl.semaphore_wait(barrier, len(peers))

    for r in range(1, X):
        send(wx.at[0], wx.at[r], wx_s.at[r], wx_r.at[r], at_x(r))
    send(call.at[x, yh], call.at[x, yh], cy_s.at[0], cy_r.at[0], at_y(YL))
    for r in range(1, X):
        send(call.at[x, yh], call.at[x, yh], ca_s.at[r], ca_r.at[r], at_x(r))

    load_t.wait()
    root = F32(width ** -0.5)
    trot[...] = (jnp.dot(tbuf[...], signs[...], preferred_element_type=F32) * root).astype(BF16)

    for r in range(1, X):
        wait_in(wx.at[r], wx_s.at[r], wx_r.at[r])
    mixed = wx[0].astype(F32) * sign(x, x)
    for r in range(1, X):
        mixed = mixed + wx[r].astype(F32) * sign(x, (x + X - r) % X)
    wy[0] = (mixed * F32(X ** -0.5)).astype(BF16)
    for r in range(1, NY):
        send(wy.at[0], wy.at[r], wy_s.at[r], wy_r.at[r], at_y(r))

    wait_in(call.at[x, 1 - yh], cy_s.at[0], cy_r.at[0])
    for r in range(1, X):
        send(call.at[x, 1 - yh], call.at[x, 1 - yh], cb_s.at[r], cb_r.at[r], at_x(r))

    for r in range(1, NY):
        wait_in(wy.at[r], wy_s.at[r], wy_r.at[r])
    for r in range(YL):
        pair = wy[r].astype(F32) * sign(yh, ((yy + NY - r) % NY) // YL)
        pair = pair + wy[r + YL].astype(F32) * sign(yh, ((yy + NY - r - YL) % NY) // YL)
        wall[z, (yl + YL - r) % YL, c] = (pair * F32(0.5 ** 0.5)).astype(BF16)
    for r in range(1, Z):
        send(wall.at[z, :, c], wall.at[z, :, c], wz_s.at[r], wz_r.at[r], at_z(r))
    send(wall.at[z, :, c], wall.at[z, :, c], wc_s.at[0], wc_r.at[0], at_core)

    for r in range(1, X):
        src = (x + X - r) % X
        wait_in(call.at[src, yh], ca_s.at[r], ca_r.at[r])
        wait_in(call.at[src, 1 - yh], cb_s.at[r], cb_r.at[r])
    for r in list(range(1, Z)) + [0]:
        zz = (z + r) % Z
        cols = call[:, :, :, pl.ds(pl.multiple_of(zz * group, group), group)]
        part = lax.dot_general(
            cols.reshape(X * YH * K, group), trot[...], (((0,), (0,)), ((), ())),
            preferred_element_type=F32,
        )
        pbuf[zz] = part.astype(BF16).reshape(YL, NC, K, width)
        send(pbuf.at[zz, :, 1 - c], pcore.at[zz], pc_s.at[r], pc_r.at[r], at_core)

    for r in range(1, Z):
        src = (z + Z - r) % Z
        wait_in(wall.at[src, :, c], wz_s.at[r], wz_r.at[r])
        send(wall.at[src, :, c], wall.at[src, :, c], wc_s.at[r], wc_r.at[r], at_core)

    for r in list(range(1, Z)) + [0]:
        zz = (z + r) % Z
        wait_in(pcore.at[zz], pc_s.at[r], pc_r.at[r])
        total = pbuf[zz, :, c].astype(F32) + pcore[zz].astype(F32)
        psum[zz] = total.astype(BF16)
        if r:
            send(psum.at[zz], prz.at[r], pz_s.at[r], pz_r.at[r], at_z(r))

    for r in range(Z):
        src = (z + Z - r) % Z
        wait_in(wall.at[src, :, 1 - c], wc_s.at[r], wc_r.at[r])
    for n in range(Z):
        part = lax.dot_general(
            trot[...], wall[n].reshape(group, width), (((1,), (1,)), ((), ())),
            preferred_element_type=F32,
        )
        obuf[:, :, :, n * group:(n + 1) * group] = part.astype(BF16).reshape(X, YH, K, group)
    for r in range(1, X):
        send(obuf.at[(x + r) % X], orx.at[r], ox_s.at[r], ox_r.at[r], at_x(r))

    half = X // 2
    for n in range(2):
        rows = call[n * half:(n + 1) * half].reshape(half * YH * K, kv)
        grad = jnp.dot(rows, wall[...].reshape(kv, width), preferred_element_type=F32)
        grad = jnp.dot(grad.astype(BF16), signs[...], preferred_element_type=F32) * root
        gbuf[n * half * YH * K:(n + 1) * half * YH * K] = grad.astype(BF16)
    store_g = pltpu.make_async_copy(gbuf, gtok, lsem.at[3])
    store_g.start()

    total = psum[z].astype(F32)
    for r in range(1, Z):
        wait_in(prz.at[r], pz_s.at[r], pz_r.at[r])
        total = total + prz[r].astype(F32)
    py[...] = total.astype(BF16)
    for r in range(1, NY):
        send(py.at[(yl + r) % YL], pry.at[r], py_s.at[r], py_r.at[r], at_y(r))

    total = obuf[x].astype(F32)
    for r in range(1, X):
        wait_in(orx.at[r], ox_s.at[r], ox_r.at[r])
        total = total + orx[r].astype(F32)
    oy[...] = total.astype(BF16)
    send(oy.at[1 - yh], ory, oy_s.at[0], oy_r.at[0], at_y(YL))

    total = py[yl].astype(F32) * sign(yh, yh)
    for r in range(1, NY):
        wait_in(pry.at[r], py_s.at[r], py_r.at[r])
        total = total + pry[r].astype(F32) * sign(yh, ((yy + NY - r) % NY) // YL)
    px[0] = total.astype(BF16)
    for r in range(1, X):
        send(px.at[0], px.at[r], px_s.at[r], px_r.at[r], at_x(r))

    wait_in(ory, oy_s.at[0], oy_r.at[0])
    obuf_out[...] = (oy[yh].astype(F32) + ory[...].astype(F32)).astype(BF16)
    store_o = pltpu.make_async_copy(obuf_out, out, lsem.at[4])
    store_o.start()

    total = px[0].astype(F32) * sign(x, x)
    for r in range(1, X):
        wait_in(px.at[r], px_s.at[r], px_r.at[r])
        total = total + px[r].astype(F32) * sign(x, (x + X - r) % X)
    gwbuf[...] = total * F32(norm * (X * YH) ** -0.5)
    store_w = pltpu.make_async_copy(gwbuf, gwgt, lsem.at[5])
    store_w.start()

    for copy in sends:
        copy.wait_send()
    store_g.wait()
    store_o.wait()
    store_w.wait()


def on_device(norm, tokens, weight, cotangent):
    rows, width = tokens.shape
    kv = cotangent.shape[1]
    vmem = pltpu.VMEM
    any_spec = pl.BlockSpec(memory_space=pl.ANY)
    dma = lambda n: pltpu.SemaphoreType.DMA((n,))
    scratch = [
        vmem((rows, width), BF16),
        vmem((rows, width), BF16),
        vmem((width, width), BF16),
        vmem((X, K, width), BF16),
        vmem((YL * YH, K, width), BF16),
        vmem((Z, YL, NC, K, width), BF16),
        vmem((X, YH, K, kv), BF16),
        vmem((Z, YL, NC, K, width), BF16),
        vmem((Z, YL, K, width), BF16),
        vmem((Z, YL, K, width), BF16),
        vmem((Z, YL, K, width), BF16),
        vmem((YL, K, width), BF16),
        vmem((YL * YH, K, width), BF16),
        vmem((X, K, width), BF16),
        vmem((X, YH, K, kv), BF16),
        vmem((X, YH, K, kv), BF16),
        vmem((YH, K, kv), BF16),
        vmem((K, kv), BF16),
        vmem((K, kv), BF16),
        vmem((rows, width), BF16),
        vmem((K, width), F32),
        dma(6),
    ]
    for n in (X, YL * YH, Z, Z, 1, X, X, Z, Z, YL * YH, X, X, 1):
        scratch += [dma(n), dma(n)]
    return pl.pallas_call(
        functools.partial(kernel, norm),
        out_shape=(
            jax.ShapeDtypeStruct((K, kv), BF16),
            jax.ShapeDtypeStruct((rows, width), BF16),
            jax.ShapeDtypeStruct((K, width), F32),
        ),
        in_specs=[any_spec] * 3,
        out_specs=(any_spec,) * 3,
        scratch_shapes=scratch,
        compiler_params=pltpu.CompilerParams(
            collective_id=0, has_side_effects=True, vmem_limit_bytes=40 * 2**20
        ),
    )(tokens, weight, cotangent)


def solution(mesh):
    assert dict(mesh.shape) == {"dp": Z * YL * NC, "tensor": X * YH}

    def whole(tokens, weight, cotangent):
        return jax.shard_map(
            functools.partial(on_device, tokens.shape[0] ** -0.5),
            mesh=mesh,
            in_specs=(P("dp", "tensor"), P("dp", "tensor"), P(("dp", "tensor"), None)),
            out_specs=(P(("dp", "tensor"), None), P("dp", "tensor"), P("dp", "tensor")),
            check_vma=False,
        )(tokens, weight, cotangent)

    return whole
```

time: 667 us -> 75.9 us (0.11)
  the two profiles are of different devices: /device:TPU:2 before, /device:TPU:4 now
where the time goes in v1:
time: 75.9 us; the launch traced here: 75.6 us
  Pallas kernels  70.6 us (93%)
  local copies, waits for them, and re-layouts  4.35 us (6%)
    pallas_call x1, Pallas kernels, on_device(): pl.pallas_call(functools.partial(kernel, norm), out_shape=(jax.ShapeDtype...  70.6 us
    unnamed x9, local copies, waits for them, and re-layouts  4.35 us

profile of v1, /device:TPU:4, one launch (start us, length us, event | category | flops | bytes accessed | tf_op | source)
XLA Modules:
  0.0 75.6 jit_solution(14161774782067249806)
XLA Ops:
  0.6 0.0 copy-start
  0.6 0.9 %copy-done = bf16[256,512]{1,0:T(8,128)(2,1)S(1)} copy-done((bf16[256,512]{1,0:T(8,128)(2,1)S(1)}, bf16[256,512]{1,0:T(8,128)(2,1)}, u32[]{:S(2)}) %copy-start) | copy-done | bytes 262168
  1.6 0.0 copy-start.1
  1.6 0.8 copy-done.1
  2.3 0.0 copy-start.2
  2.3 0.7 copy-done.2
  3.1 70.6 %shard_map.58 = (bf16[16,1024]{1,0:T(8,128)(2,1)S(1)}, bf16[256,512]{1,0:T(8,128)(2,1)S(1)}, f32[16,512]{1,0:T(8,128)S(1)}) custom-call(bf16[256,512]{1,0:T(8,128)(2,1)S(1)} %copy-done, bf16[16,512]{1,0:T(8,128)(2,1)S(1)} %copy-done.2, bf16[16,1024]{1,0:T(8,128)(2,1)S(1)} %copy-done.1), custom_call_target="tpu_custom_call" | custom-call | tf_op jit(solution)/shard_map/pallas_call | solution.py:256
  73.7 0.6 copy.9
  74.3 0.7 copy.10
  75.0 0.6 copy.11
Async XLA Ops:
  0.6 1.0 %copy-start = (bf16[256,512]{1,0:T(8,128)(2,1)S(1)}, bf16[256,512]{1,0:T(8,128)(2,1)}, u32[]{:S(2)}) copy-start(bf16[256,512]{1,0:T(8,128)(2,1)} %tok.1) | copy-start | bytes 786436
  1.6 0.8 %copy-start.1 = (bf16[16,1024]{1,0:T(8,128)(2,1)S(1)}, bf16[16,1024]{1,0:T(8,128)(2,1)}, u32[]{:S(2)}) copy-start(bf16[16,1024]{1,0:T(8,128)(2,1)} %cot.1) | copy-start | bytes 98308
  2.3 0.7 copy-start.2

commit v2 on v1

v2 whole, which is shorter than its diff:
```python
import functools

import jax
import jax.numpy as jnp
from jax import lax
from jax.experimental import pallas as pl
from jax.experimental.pallas import tpu as pltpu
from jax.sharding import PartitionSpec as P

Z, YL, NC = 8, 4, 2
X, YH = 8, 2
K = 16
WZD, PZD, CD, WF = True, False, True, False
WZD, PZD, ORD, CD, WF = True, True, 1, False, True
ZO = (4, 3, 5, 2, 6, 1, 7)
F32, BF16 = jnp.float32, jnp.bfloat16


def signs_table(width):
    bits = lax.broadcasted_iota(jnp.int32, (width, width), 0) & lax.broadcasted_iota(
        jnp.int32, (width, width), 1
    )
    for shift in (8, 4, 2, 1):
        bits = bits ^ (bits >> shift)
    return (1 - 2 * (bits & 1)).astype(F32).astype(BF16)


def sign(a, b):
    bits = a & b
    bits = bits ^ (bits >> 2)
    bits = bits ^ (bits >> 1)
    return (1 - 2 * (bits & 1)).astype(F32)


def kernel(
    norm,
    tok, wgt, cot,
    out, gtok, gwgt,
    tbuf, trot, signs, wx, wy, wall, call, pbuf, pcore, psum, prz, pnear, pfar, pmid, pfin, py, pry, px,
    obuf, onear, ofar, omid, ofin, oy, ory, obuf_out, gbuf, gwbuf,
    lsem, wx_s, wx_r, wy_s, wy_r, wz_s, wz_r, wf_s, wc_s, wc_r, cy_s, cy_r, ca_s, ca_r, cb_s, cb_r,
    pc_s, pc_r, pz_s, pz_r, py_s, py_r, px_s, px_r, ox_s, ox_r, oy_s, oy_r,
):
    width = tbuf.shape[1]
    group = YL * NC * K
    rows = X * YH * K
    d, t = lax.axis_index("dp"), lax.axis_index("tensor")
    z, yl, c = d // (YL * NC), (d // NC) % YL, d % NC
    x, yh = t // YH, t % YH
    yy = yh * YL + yl
    NY = YL * YH
    kv = cot.shape[1]

    def at_x(r):
        return {"dp": d, "tensor": ((x + r) % X) * YH + yh}

    def at_z(r):
        return {"dp": (((z + r) % Z) * YL + yl) * NC + c, "tensor": t}

    def at_y(r):
        v = (yy + r) % NY
        return {"dp": (z * YL + v % YL) * NC + c, "tensor": x * YH + v // YL}

    at_core = {"dp": (z * YL + yl) * NC + (1 - c), "tensor": t}

    def remote(src, dst, s, r, where):
        return pltpu.make_async_remote_copy(
            src_ref=src, dst_ref=dst, send_sem=s, recv_sem=r,
            device_id=where, device_id_type=pl.DeviceIdType.MESH,
        )

    sends = []

    def send(src, dst, s, r, where):
        copy = remote(src, dst, s, r, where)
        copy.start()
        sends.append(copy)

    def wait_in(dst, s, r):
        remote(dst, dst, s, r, at_core).wait_recv()

    load_w = pltpu.make_async_copy(wgt, wx.at[0], lsem.at[0])
    load_w.start()
    load_c = pltpu.make_async_copy(cot, call.at[x, yh], lsem.at[5])
    load_c.start()
    load_t = pltpu.make_async_copy(tok, tbuf, lsem.at[1])
    load_t.start()

    peers = (
        [at_x(r) for r in range(1, X)]
        + [at_y(r) for r in range(1, NY)]
        + [at_z(r) for r in range(1, Z)]
        + [at_core]
    )
    barrier = pltpu.get_barrier_semaphore()
    for peer in peers:
        pl.semaphore_signal(barrier, inc=1, device_id=peer, device_id_type=pl.DeviceIdType.MESH)
    signs[...] = signs_table(width)
    load_w.wait()
    load_c.wait()
    pl.semaphore_wait(barrier, len(peers))

    for r in range(1, X):
        send(wx.at[0], wx.at[r], wx_s.at[r], wx_r.at[r], at_x(r))
    own = call.at[x, yh]
    send(own, own, cy_s.at[0], cy_r.at[0], at_y(YL))
    near = (4, 3, 5, 2, 6, 1, 7) if CD else (2, X - 2, 1, X - 1)
    for r in near:
        send(own, own, ca_s.at[r], ca_r.at[r], at_x(r))

    load_t.wait()
    root = F32(width ** -0.5)
    trot[...] = (jnp.dot(tbuf[...], signs[...], preferred_element_type=F32) * root).astype(BF16)

    def pass_on(h, s, r, far):
        if CD:
            return
        for came, step in ((2, 1), (X - 2, X - 1)):
            piece = call.at[(x + X - came) % X, h]
            wait_in(piece, s.at[came], r.at[came])
            to = (came + step) % X
            send(piece, piece, s.at[to], r.at[to], at_x(step))
            if came == far:
                send(piece, piece, s.at[X // 2], r.at[X // 2], at_x(far))

    if not WF:
        pass_on(yh, ca_s, ca_r, 2)

    other = call.at[x, 1 - yh]
    wait_in(other, cy_s.at[0], cy_r.at[0])
    for r in near:
        send(other, other, cb_s.at[r], cb_r.at[r], at_x(r))

    for r in range(1, X):
        wait_in(wx.at[r], wx_s.at[r], wx_r.at[r])
    mixed = wx[0].astype(F32) * sign(x, x)
    for r in range(1, X):
        mixed = mixed + wx[r].astype(F32) * sign(x, (x + X - r) % X)
    wy[0] = (mixed * F32(X ** -0.5)).astype(BF16)
    for r in range(1, NY):
        send(wy.at[0], wy.at[r], wy_s.at[r], wy_r.at[r], at_y(r))

    if WF:
        pass_on(yh, ca_s, ca_r, 2)
    pass_on(1 - yh, cb_s, cb_r, X - 2)

    for r in range(1, NY):
        wait_in(wy.at[r], wy_s.at[r], wy_r.at[r])
    for r in range(YL):
        pair = wy[r].astype(F32) * sign(yh, ((yy + NY - r) % NY) // YL)
        pair = pair + wy[r + YL].astype(F32) * sign(yh, ((yy + NY - r - YL) % NY) // YL)
        wall[z, (yl + YL - r) % YL, c] = (pair * F32(0.5 ** 0.5)).astype(BF16)
    mine = wall.at[z, :, c]
    for r in (ZO if WZD else (2, Z - 2, 1, Z - 1)):
        send(mine, mine, wz_s.at[r], wz_r.at[r], at_z(r))
    remote(mine, mine, wc_s.at[z], wc_r.at[z], at_core).start()

    mid = YL // 2

    def pass_up(n):
        piece, part = wall.at[n, :, c], wall.at[n, pl.ds(0, mid), c]
        remote(piece, piece, wf_s.at[0], wz_r.at[3], at_z(1)).start()
        remote(part, part, wf_s.at[1], wz_r.at[4], at_z(2)).start()

    def pass_down(n):
        piece, part = wall.at[n, :, c], wall.at[n, pl.ds(mid, mid), c]
        remote(piece, piece, wf_s.at[2], wz_r.at[5], at_z(Z - 1)).start()
        remote(part, part, wf_s.at[3], wz_r.at[0], at_z(Z - 2)).start()

    @(lambda f: None if WZD else pl.when((z >= 2))(f))
    def _():
        n = (z + Z - 2) % Z
        wait_in(wall.at[n, :, c], wz_s.at[2], wz_r.at[2])
        pass_up(n)

    @(lambda f: None if WZD else pl.when((z >= Z - 2))(f))
    def _():
        n = (z + 2) % Z
        wait_in(wall.at[n, :, c], wz_s.at[Z - 2], wz_r.at[Z - 2])
        pass_down(n)

    for r in (range(1, X) if CD else (1, 3, 4, 5, 7)):
        src = (x + X - r) % X
        wait_in(call.at[src, yh], ca_s.at[r], ca_r.at[r])
        wait_in(call.at[src, 1 - yh], cb_s.at[r], cb_r.at[r])
    order = (3, 5, 4, 1, 7, 2, 6, 0)
    for r in order:
        first = pl.multiple_of(((z + r) % Z) * group, group)
        part = lax.dot_general(
            call[:, :, :, pl.ds(first, group)].reshape(rows, group), trot[...],
            (((0,), (0,)), ((), ())), preferred_element_type=F32,
        )
        pbuf[r] = part.astype(BF16).reshape(YL, NC, K, width)
        send(pbuf.at[r, :, 1 - c], pcore.at[r], pc_s.at[r], pc_r.at[r], at_core)
    low, high = pl.ds(0, mid), pl.ds(mid, mid)
    for r in order:
        wait_in(pcore.at[r], pc_s.at[r], pc_r.at[r])
        psum[r] = (pbuf[r, :, c].astype(F32) + pcore[r].astype(F32)).astype(BF16)
        if PZD:
            if r:
                send(psum.at[r], prz.at[r], pz_s.at[r], pz_r.at[r], at_z(r))
        elif r == 3:
            send(psum.at[r], pnear.at[0], pz_s.at[0], pz_r.at[0], at_z(1))
        elif r == 5:
            send(psum.at[r], pnear.at[1], pz_s.at[1], pz_r.at[1], at_z(Z - 1))
        elif r == 4:
            send(psum.at[r, low], pfar.at[0], pz_s.at[2], pz_r.at[2], at_z(2))
            send(psum.at[r, high], pfar.at[1], pz_s.at[3], pz_r.at[3], at_z(Z - 2))
        elif r == 1:
            send(psum.at[r], pfin.at[0], pz_s.at[4], pz_r.at[4], at_z(1))
        elif r == 7:
            send(psum.at[r], pfin.at[1], pz_s.at[5], pz_r.at[5], at_z(Z - 1))

    @(lambda f: None if WZD else pl.when((z < Z - 2))(f))
    def _():
        n = z + 2
        wait_in(wall.at[n, :, c], wz_s.at[Z - 2], wz_r.at[Z - 2])
        pass_down(n)

    @(lambda f: None if WZD else pl.when((z < 2))(f))
    def _():
        n = z + Z - 2
        wait_in(wall.at[n, :, c], wz_s.at[2], wz_r.at[2])
        pass_up(n)

    def sum_on():
        if PZD:
            return
        for e, r in enumerate((2, Z - 2)):
            wait_in(pnear.at[e], pz_s.at[e], pz_r.at[e])
            wait_in(pfar.at[e], pz_s.at[2 + e], pz_r.at[2 + e])
            total = psum[r].astype(F32) + pnear[e].astype(F32)
            for n in range(YL):
                v = total[n]
                if n // mid == e:
                    v = v + pfar[e, n % mid].astype(F32)
                pmid[e, n] = v.astype(BF16)
            send(pmid.at[e], pfin.at[2 + e], pz_s.at[6 + e], pz_r.at[6 + e], at_z(r))

    bounds = (0, 4, 6, 8)
    spans = list(zip(bounds[:-1], bounds[1:]))

    def keys(g):
        lo, hi = spans[g]
        for n in range(lo, hi):
            r = (z + Z - n) % Z
            piece = wall.at[n, :, c]
            held = (r == 0) if WZD else (r == 0) | (r == 2) | (r == Z - 2)

            @pl.when(jnp.logical_not(held) if WZD else jnp.logical_not(held) & (r != Z // 2))
            def _():
                wait_in(piece, wz_s.at[r], wz_r.at[r])

            @(lambda f: None if WZD else pl.when(r == Z // 2)(f))
            def _():
                wait_in(wall.at[n, pl.ds(0, mid), c], wz_s.at[4], wz_r.at[4])
                wait_in(wall.at[n, pl.ds(mid, mid), c], wz_s.at[0], wz_r.at[0])

            @pl.when(z != n)
            def _():
                remote(piece, piece, wc_s.at[n], wc_r.at[n], at_core).start()

        for n in range(lo, hi):
            wait_in(wall.at[n, :, 1 - c], wc_s.at[n], wc_r.at[n])
            part = lax.dot_general(
                trot[...], wall[n].reshape(group, width), (((1,), (1,)), ((), ())),
                preferred_element_type=F32,
            )
            obuf[n] = part.astype(BF16).reshape(X, YH, K, group)
        span = pl.ds(lo, hi - lo)
        ahead, behind, across = (x + 3) % X, (x + X - 3) % X, (x + X // 2) % X
        s, r = ox_s.at[g], ox_r.at[g]
        send(obuf.at[span, ahead], onear.at[0, span], s.at[0], r.at[0], at_x(1))
        send(obuf.at[span, behind], onear.at[1, span], s.at[1], r.at[1], at_x(X - 1))
        send(obuf.at[span, across, 0], ofar.at[0, span], s.at[2], r.at[2], at_x(2))
        send(obuf.at[span, across, 1], ofar.at[1, span], s.at[3], r.at[3], at_x(X - 2))
        send(obuf.at[span, (x + 1) % X], ofin.at[0, span], s.at[4], r.at[4], at_x(1))
        send(obuf.at[span, (x + X - 1) % X], ofin.at[1, span], s.at[5], r.at[5], at_x(X - 1))

    def keys_on(g):
        lo, hi = spans[g]
        span = pl.ds(lo, hi - lo)
        s, q = ox_s.at[g], ox_r.at[g]
        for e, r in enumerate((2, X - 2)):
            wait_in(onear.at[e, span], s.at[e], q.at[e])
            wait_in(ofar.at[e, span], s.at[2 + e], q.at[2 + e])
            total = obuf[lo:hi, (x + r) % X].astype(F32) + onear[e, lo:hi].astype(F32)
            for h in range(YH):
                v = total[:, h]
                if h == e:
                    v = v + ofar[e, lo:hi].astype(F32)
                omid[e, lo:hi, h] = v.astype(BF16)
            send(omid.at[e, span], ofin.at[2 + e, span], s.at[6 + e], q.at[6 + e], at_x(r))

    def keys_sum(g):
        lo, hi = spans[g]
        total = obuf[lo:hi, x].astype(F32)
        for e in range(4):
            wait_in(ofin.at[e, pl.ds(lo, hi - lo)], ox_s.at[g].at[4 + e], ox_r.at[g].at[4 + e])
            total = total + ofin[e, lo:hi].astype(F32)
        for h in range(YH):
            oy[h, lo:hi] = total[:, h].astype(BF16)
        span = pl.ds(lo, hi - lo)
        send(oy.at[1 - yh, span], ory.at[span], oy_s.at[g], oy_r.at[g], at_y(YL))

    def planes_sum():
        total = psum[0].astype(F32)
        if PZD:
            for r in range(1, Z):
                wait_in(prz.at[r], pz_s.at[r], pz_r.at[r])
                total = total + prz[r].astype(F32)
        else:
            for e in range(4):
                wait_in(pfin.at[e], pz_s.at[4 + e], pz_r.at[4 + e])
                total = total + pfin[e].astype(F32)
        py[...] = total.astype(BF16)
        for r in range(1, NY):
            send(py.at[(yl + r) % YL], pry.at[r], py_s.at[r], py_r.at[r], at_y(r))

    def rows_sum():
        total = py[yl].astype(F32) * sign(yh, yh)
        for r in range(1, NY):
            wait_in(pry.at[r], py_s.at[r], py_r.at[r])
            total = total + pry[r].astype(F32) * sign(yh, ((yy + NY - r) % NY) // YL)
        px[0] = total.astype(BF16)
        for r in range(1, X):
            send(px.at[0], px.at[r], px_s.at[r], px_r.at[r], at_x(r))

    keys(0)
    sum_on()
    keys(1)
    keys_on(0)
    keys(2)
    keys_on(1)
    planes_sum()
    keys_on(2)
    rows_sum()
    keys_sum(0)
    keys_sum(1)

    for n in range(2):
        lo, hi = n * (X // 2), (n + 1) * (X // 2)
        grad = jnp.dot(
            call[lo:hi].reshape(rows // 2, kv), wall[...].reshape(kv, width),
            preferred_element_type=F32,
        )
        grad = jnp.dot(grad.astype(BF16), signs[...], preferred_element_type=F32) * root
        gbuf[n * (rows // 2):(n + 1) * (rows // 2)] = grad.astype(BF16)
    store_g = pltpu.make_async_copy(gbuf, gtok, lsem.at[2])
    store_g.start()

    keys_sum(2)

    total = px[0].astype(F32) * sign(x, x)
    for r in range(1, X):
        wait_in(px.at[r], px_s.at[r], px_r.at[r])
        total = total + px[r].astype(F32) * sign(x, (x + X - r) % X)
    gwbuf[...] = total * F32(norm * (X * YH) ** -0.5)
    store_w = pltpu.make_async_copy(gwbuf, gwgt, lsem.at[4])
    store_w.start()

    for g, (lo, hi) in enumerate(spans):
        wait_in(ory.at[pl.ds(lo, hi - lo)], oy_s.at[g], oy_r.at[g])
    for n in range(Z):
        both = oy[yh, n].astype(F32) + ory[n].astype(F32)
        obuf_out[:, n * group:(n + 1) * group] = both.astype(BF16)
    store_o = pltpu.make_async_copy(obuf_out, out, lsem.at[3])
    store_o.start()

    for copy in sends:
        copy.wait_send()
    for n in range(Z):
        piece = wall.at[n, :, c]
        remote(piece, piece, wc_s.at[n], wc_r.at[n], at_core).wait_send()
    for e, part in () if WZD else enumerate((pl.ds(0, YL), low, pl.ds(0, YL), high)):
        piece = wall.at[z, part, c]
        remote(piece, piece, wf_s.at[e], wz_r.at[e], at_core).wait_send()
    store_g.wait()
    store_o.wait()
    store_w.wait()


def on_device(norm, tokens, weight, cotangent):
    rows, width = tokens.shape
    kv = cotangent.shape[1]
    vmem = pltpu.VMEM
    any_spec = pl.BlockSpec(memory_space=pl.ANY)
    dma = lambda n: pltpu.SemaphoreType.DMA(n if isinstance(n, tuple) else (n,))
    group = YL * NC * K
    scratch = [
        vmem((rows, width), BF16),
        vmem((rows, width), BF16),
        vmem((width, width), BF16),
        vmem((X, K, width), BF16),
        vmem((YL * YH, K, width), BF16),
        vmem((Z, YL, NC, K, width), BF16),
        vmem((X, YH, K, kv), BF16),
        vmem((Z, YL, NC, K, width), BF16),
        vmem((Z, YL, K, width), BF16),
        vmem((Z, YL, K, width), BF16),
        vmem((Z, YL, K, width), BF16),
        vmem((2, YL, K, width), BF16),
        vmem((2, YL // 2, K, width), BF16),
        vmem((2, YL, K, width), BF16),
        vmem((4, YL, K, width), BF16),
        vmem((YL, K, width), BF16),
        vmem((YL * YH, K, width), BF16),
        vmem((X, K, width), BF16),
        vmem((Z, X, YH, K, group), BF16),
        vmem((2, Z, YH, K, group), BF16),
        vmem((2, Z, K, group), BF16),
        vmem((2, Z, YH, K, group), BF16),
        vmem((4, Z, YH, K, group), BF16),
        vmem((YH, Z, K, group), BF16),
        vmem((Z, K, group), BF16),
        vmem((K, kv), BF16),
        vmem((rows, width), BF16),
        vmem((K, width), F32),
        dma(6),
    ]
    for n in (X, YL * YH, Z):
        scratch += [dma(n), dma(n)]
    scratch += [dma(4)]
    for n in (Z, 1, X, X, Z, 8, YL * YH, X, (3, 8), 3):
        scratch += [dma(n), dma(n)]
    return pl.pallas_call(
        functools.partial(kernel, norm),
        out_shape=(
            jax.ShapeDtypeStruct((K, kv), BF16),
            jax.ShapeDtypeStruct((rows, width), BF16),
            jax.ShapeDtypeStruct((K, width), F32),
        ),
        in_specs=[pl.BlockSpec(memory_space=pltpu.HBM)] * 3,
        out_specs=(any_spec,) * 3,
        scratch_shapes=scratch,
        compiler_params=pltpu.CompilerParams(
            collective_id=0, has_side_effects=True, vmem_limit_bytes=63 * 2**20
        ),
    )(tokens, weight, cotangent)


def solution(mesh):
    assert dict(mesh.shape) == {"dp": Z * YL * NC, "tensor": X * YH}

    def whole(tokens, weight, cotangent):
        return jax.shard_map(
            functools.partial(on_device, tokens.shape[0] ** -0.5),
            mesh=mesh,
            in_specs=(P("dp", "tensor"), P("dp", "tensor"), P(("dp", "tensor"), None)),
            out_specs=(P(("dp", "tensor"), None), P("dp", "tensor"), P("dp", "tensor")),
            check_vma=False,
        )(tokens, weight, cotangent)

    return whole
```

time: 75.9 us -> 74.6 us (0.983)
  the two profiles are of different devices: /device:TPU:4 before, /device:TPU:128 now
where the time goes in v2:
time: 74.6 us; the launch traced here: 74.3 us
  Pallas kernels  70 us (94%)
  local copies, waits for them, and re-layouts  3.67 us (5%)
    pallas_call x1, Pallas kernels, on_device(): pl.pallas_call(functools.partial(kernel, norm), out_shape=(jax.ShapeDtype...  70 us
    unnamed x5, local copies, waits for them, and re-layouts  3.67 us

profile of v2, /device:TPU:128, one launch (start us, length us, event | category | flops | bytes accessed | tf_op | source)
XLA Modules:
  0.0 74.3 jit_solution(2360858163073333842)
XLA Ops:
  0.6 70.0 %shard_map.58 = (bf16[16,1024]{1,0:T(8,128)(2,1)}, bf16[256,512]{1,0:T(8,128)(2,1)}, f32[16,512]{1,0:T(8,128)}) custom-call(bf16[256,512]{1,0:T(8,128)(2,1)} %tok.1, bf16[16,512]{1,0:T(8,128)(2,1)} %wgt.1, bf16[16,1024]{1,0:T(8,128)(2,1)} %cot.1), custom_call_target="tpu_custom_call" | custom-call | tf_op jit(solution)/shard_map/pallas_call | solution.py:426
  70.7 1.4 %copy.9 = bf16[16,1024]{1,0:T(8,128)(2,1)} copy(bf16[16,1024]{1,0:T(8,128)(2,1)} %get-tuple-element.6) | data formatting | bytes 65536
  72.0 0.0 copy-start
  72.1 1.7 %copy.10 = bf16[256,512]{1,0:T(8,128)(2,1)} copy(bf16[256,512]{1,0:T(8,128)(2,1)} %get-tuple-element.7) | data formatting | bytes 524288
  73.7 0.0 copy-done
  73.7 0.6 copy.11
Async XLA Ops:
  72.0 1.7 %copy-start = (f32[16,512]{1,0:T(8,128)S(1)}, f32[16,512]{1,0:T(8,128)}, u32[]{:S(2)}) copy-start(f32[16,512]{1,0:T(8,128)} %get-tuple-element.8) | copy-start | bytes 98308
